TPU v7x, 32 devices: a whole 2x2x4 slice. The times are simulated.
32 devices in a mesh: parts: 2 (over x), grp: 2 (over core), pan: 8 (over z, y).
Axes of the slice: x: 2, y: 2, z: 4, core: 2. Of those that a mesh axis runs over, the one named last changes fastest.
Arguments:
- surface_field: float32 [1536, 2, 16, 128], P(('parts', 'grp', 'pan')), parts along dimension 0, may hold values from -6 to 6
- positions: bfloat16 [1536, 3, 128], P(('parts', 'grp', 'pan')), parts along dimension 0, may hold values from 0 to 1
- quad_weight: float32 [1536, 128], P(('parts', 'grp', 'pan')), parts along dimension 0, may hold values from 0.2 to 1
- octree_order: int32 [32, 48], P(('parts', 'grp', 'pan')), parts along dimension 0, may hold values from 0 to 47, each once within a row
- near_target: int32 [32, 144], P('parts'), parts along dimension 0, may hold values from 0 to 47
- near_source: int32 [32, 144], P('parts'), parts along dimension 0, may hold values from 0 to 143
- near_count: int32 [32], P('parts'), parts along dimension 0, may hold values from 36 to 144, as said below
- compress: bfloat16 [1536, 128, 128], P(('parts', 'grp', 'pan')), parts along dimension 0, may hold values from -0.375 to 0.375
- expand: bfloat16 [1536, 64, 256], P(('parts', 'grp', 'pan')), parts along dimension 0, may hold values from -0.5 to 0.5
- mixing: bfloat16 [4, 768, 2, 2, 64, 128], P(None, ('parts', 'grp', 'pan')), parts along dimension 1, may hold values from -0.375 to 0.375
Outputs:
- operator_image: float32 [1536, 2, 16, 128], P(('parts', 'grp', 'pan')), parts along dimension 0
There are 2 independent parts, one for each index of `parts`. A program takes and returns all parts, laid end to end along the dimension named above; each array names one. Nothing has to cross between parts.
Inputs may be any that keep to these rules, and one draw needn't show every extreme that they name: `octree_order`: each row is a permutation of the panel slots. `near_count`: pair slots from the count on are ignored; some device has exactly 144 live pairs.
All inputs are finite; a program needn't handle non-finite values.
Results may differ from a plain program's by a relative error of at most 0.0048.
Values may be sent and summed in bfloat16 or wider, within the bound.
A program may use at most 64 MiB of HBM per device.

v0:
```python
import math

import jax
import jax.numpy as jnp
from jax import lax
from jax.sharding import PartitionSpec as P

wavenumber = 6.0
softening = 0.05


def padded(block, sides, width):
    for axis, dim in sides:
        count = lax.axis_size(axis)
        forward = [(i, i + 1) for i in range(count - 1)]
        backward = [(target, source) for source, target in forward]
        low = lax.ppermute(
            lax.slice_in_dim(block, block.shape[dim] - width, None, axis=dim), axis, forward
        )
        high = lax.ppermute(lax.slice_in_dim(block, 0, width, axis=dim), axis, backward)
        block = jnp.concatenate([low, block, high], axis=dim)
    return block


def partner(x, axis, stride):
    return lax.ppermute(x, axis, [(i, i ^ 1 << stride) for i in range(lax.axis_size(axis))])


def one_hot_rows(row_ids, table_rows, dtype):
    return (row_ids[:, None] == jnp.arange(table_rows, dtype=jnp.int32)[None, :]).astype(dtype)


def select_rows(table, row_ids):
    selector = one_hot_rows(row_ids, table.shape[0], table.dtype)
    flat_table = table.reshape(table.shape[0], -1)
    picked = jnp.dot(selector, flat_table, preferred_element_type=jnp.float32).astype(table.dtype)
    return picked.reshape((row_ids.shape[0],) + table.shape[1:])


def place_rows(values, row_ids, table_rows):
    selector = one_hot_rows(row_ids, table_rows, jnp.float32)
    flat_values = values.reshape(values.shape[0], -1)
    placed = jnp.dot(
        selector.T, flat_values, preferred_element_type=jnp.float32, precision=lax.Precision.HIGHEST
    )
    return placed.reshape((table_rows,) + values.shape[1:])


def pair_kernels(src_points, tgt_points):
    offsets = (
        src_points.astype(jnp.float32)[:, :, :, None]
        - tgt_points.astype(jnp.float32)[:, :, None, :]
    )
    distance = jnp.sqrt(jnp.sum(offsets * offsets, axis=1) + softening * softening)
    amplitude = 1.0 / (4.0 * math.pi * distance)
    kernel_tiles = jnp.concatenate(
        [amplitude * jnp.cos(wavenumber * distance), amplitude * jnp.sin(wavenumber * distance)], -1
    )
    return kernel_tiles.astype(jnp.bfloat16)


def complex_apply(values, kernel_tiles):
    products = jnp.einsum(
        "gcrb,gbm->gcrm", values, kernel_tiles, preferred_element_type=jnp.float32
    )
    tile_width = kernel_tiles.shape[1]
    real_out = products[:, 0, :, :tile_width] - products[:, 1, :, tile_width:]
    imag_out = products[:, 0, :, tile_width:] + products[:, 1, :, :tile_width]
    return jnp.stack([real_out, imag_out], 1)


def near_block(win_src, win_pts, tgt_pts, targets, sources, lower_slot, upper_slot):
    most_pairs = targets.shape[0]
    pair_group = math.gcd(most_pairs, 8)
    target_rows = tgt_pts.shape[0]
    accumulated = jnp.zeros((target_rows,) + win_src.shape[1:], jnp.float32)

    def step(step_index, accumulated):
        first_slot = step_index * pair_group
        tgt_rows = lax.dynamic_slice_in_dim(targets, first_slot, pair_group)
        src_rows = lax.dynamic_slice_in_dim(sources, first_slot, pair_group)
        slot_ids = first_slot + jnp.arange(pair_group, dtype=jnp.int32)
        live_mask = ((slot_ids >= lower_slot) & (slot_ids < upper_slot)).astype(jnp.float32)
        kernel_tiles = pair_kernels(select_rows(win_pts, src_rows), select_rows(tgt_pts, tgt_rows))
        pair_terms = (
            complex_apply(select_rows(win_src, src_rows), kernel_tiles)
            * live_mask[:, None, None, None]
        )
        return accumulated + place_rows(pair_terms, tgt_rows, target_rows)

    return lax.fori_loop(
        lower_slot // pair_group, (upper_slot + pair_group - 1) // pair_group, step, accumulated
    )


def butterfly_mix(stacked, weights):
    rank_width = weights.shape[3]
    real_part = jnp.einsum(
        "ihrk,hoikm->ohrm", stacked[..., :rank_width], weights, preferred_element_type=jnp.float32
    )
    imag_part = jnp.einsum(
        "ihrk,hoikm->ohrm", stacked[..., rank_width:], weights, preferred_element_type=jnp.float32
    )
    mixed_out = jnp.concatenate(
        [
            real_part[..., :rank_width] - imag_part[..., rank_width:],
            real_part[..., rank_width:] + imag_part[..., :rank_width],
        ],
        -1,
    )
    return mixed_out.reshape(-1, mixed_out.shape[2], mixed_out.shape[3]).astype(jnp.bfloat16)


def on_device(
    surface_field,
    positions,
    quad_weight,
    octree_order,
    near_target,
    near_source,
    near_count,
    compress,
    expand,
    mixing,
):
    panels = surface_field.shape[0]
    half_slots = panels // 2
    rank_width = compress.shape[2] // 2
    panel_width = expand.shape[2] // 2
    octree_rows = octree_order[0]
    sources = select_rows(
        (surface_field * quad_weight[:, None, None, :]).astype(jnp.bfloat16), octree_rows
    )
    points = select_rows(positions, octree_rows)
    win_src, win_pts = (
        padded(sources, ((("grp", "pan"), 0),), panels),
        padded(points, ((("grp", "pan"), 0),), panels),
    )
    spread = lax.axis_size("pan")
    group_index = lax.axis_index("grp")
    panel_index = lax.axis_index("pan")
    device = group_index * spread + panel_index
    near_part = near_block(
        win_src, win_pts, points, near_target[device], near_source[device], 0, near_count[device]
    )
    spectrum = jnp.einsum("pcrb,pbm->pcrm", sources, compress, preferred_element_type=jnp.float32)
    coeffs = jnp.concatenate(
        [
            spectrum[:, 0, :, :rank_width] - spectrum[:, 1, :, rank_width:],
            spectrum[:, 0, :, rank_width:] + spectrum[:, 1, :, :rank_width],
        ],
        -1,
    ).astype(jnp.bfloat16)
    top_bit = spread.bit_length() - 1
    for level in range(mixing.shape[0]):
        if level == 0:
            side_bit = group_index
        else:
            side_bit = jnp.right_shift(panel_index, top_bit - level) & 1
        outgoing = jnp.where(side_bit == 1, coeffs[:half_slots], coeffs[half_slots:])
        kept_half = jnp.where(side_bit == 1, coeffs[half_slots:], coeffs[:half_slots])
        if level == 0:
            incoming = partner(outgoing, "grp", 0)
        else:
            incoming = partner(outgoing, "pan", top_bit - level)
        low_half = jnp.where(side_bit == 1, incoming, kept_half)
        high_half = jnp.where(side_bit == 1, kept_half, incoming)
        coeffs = butterfly_mix(jnp.stack([low_half, high_half], 0), mixing[level])
    real_part = jnp.einsum(
        "prk,pkm->prm", coeffs[..., :rank_width], expand, preferred_element_type=jnp.float32
    )
    imag_part = jnp.einsum(
        "prk,pkm->prm", coeffs[..., rank_width:], expand, preferred_element_type=jnp.float32
    )
    far_part = jnp.stack(
        [
            real_part[..., :panel_width] - imag_part[..., panel_width:],
            real_part[..., panel_width:] + imag_part[..., :panel_width],
        ],
        1,
    )
    summed = near_part + far_part
    return place_rows(summed, octree_rows, panels)


def solution(mesh):
    placed = (
        P(("parts", "grp", "pan"), None, None, None),
        P(("parts", "grp", "pan"), None, None),
        P(("parts", "grp", "pan"), None),
        P(("parts", "grp", "pan"), None),
        P("parts", None),
        P("parts", None),
        P("parts"),
        P(("parts", "grp", "pan"), None, None),
        P(("parts", "grp", "pan"), None, None),
        P(None, ("parts", "grp", "pan"), None, None, None, None),
    )
    return jax.shard_map(
        on_device,
        mesh=mesh,
        in_specs=placed,
        out_specs=P(("parts", "grp", "pan"), None, None, None),
        check_vma=False,
    )
```

profile of v0, /device:TPU:2, one launch (start us, length us, event | category | flops | bytes accessed | tf_op | source)
XLA Modules:
  0.0 181.6 jit_solution(8466403193623138746)
XLA Ops:
  0.0 1.4 multiply_convert_fusion.2
  3.5 4.2 %collective-permute-start = (bf16[48,2,16,128]{3,2,1,0:T(8,128)(2,1)S(1)}, bf16[48,2,16,128]{3,2,1,0:T(8,128)(2,1)}, u32[]{:S(2)}, u32[]{:S(2)}) collective-permute-start(bf16[48,2,16,128]{3,2,1,0:T(8,128)(2,1)S(1)} %bitcast.323), channel_id=1, source_target_pairs={{0,1},{1,2},{2,3},{3,4},{4,5},{5,6},{6,7},{7,8},{8,9},{9,10},{10,1... | collective-permute-start | bytes 1179656 | tf_op jit(solution)/shard_map/ppermute | solution.py:17
  7.7 1.3 collective-permute-start.1
  9.3 1.8 fusion.45
  11.1 1.8 fusion.48
  13.3 4.0 %collective-permute-start.5 = (bf16[24,16,128]{2,1,0:T(8,128)(2,1)S(1)}, bf16[24,16,128]{2,1,0:T(8,128)(2,1)S(1)}, u32[]{:S(2)}, u32[]{:S(2)}) collective-permute-start(bf16[24,16,128]{2,1,0:T(8,128)(2,1)S(1)} %get-tuple-element.76), channel_id=1, source_target_pairs={{0,4},{1,5},{2,6},{3,7},{4,0},{5,1},{6,2},{7,3},{8,12},{9,13},{10,... | collective-permute-start | bytes 294920 | tf_op jit(solution)/shard_map/ppermute | solution.py:26
  17.5 2.5 %collective-permute-start.2 = (bf16[48,3,128]{2,1,0:T(4,128)(2,1)S(1)}, bf16[48,3,128]{2,1,0:T(4,128)(2,1)S(1)}, u32[]{:S(2)}, u32[]{:S(2)}) collective-permute-start(bf16[48,3,128]{2,1,0:T(4,128)(2,1)S(1)} %reshape.91), channel_id=1, source_target_pairs={{0,1},{1,2},{2,3},{3,4},{4,5},{5,6},{6,7},{7,8},{8,9},{9,10},{10,1... | collective-permute-start | bytes 110600 | tf_op jit(solution)/shard_map/ppermute | solution.py:17
  20.1 1.3 collective-permute-start.3
  22.6 3.8 %collective-permute-done.5 = bf16[24,16,128]{2,1,0:T(8,128)(2,1)S(1)} collective-permute-done((bf16[24,16,128]{2,1,0:T(8,128)(2,1)S(1)}, bf16[24,16,128]{2,1,0:T(8,128)(2,1)S(1)}, u32[]{:S(2)}, u32[]{:S(2)}) %collective-permute-start.5) | collective-permute-done | bytes 98336 | tf_op jit(solution)/shard_map/ppermute | solution.py:26
  26.7 1.8 fusion.51
  28.5 1.9 %fusion.54 = f32[2,24,16,128]{3,2,0,1:T(8,128)S(1)} fusion(bf16[4,24,2,2,64,128]{5,4,3,2,1,0:T(8,128)(2,1)} %param.21, bf16[2,24,16,64,1]{3,2,1,0,4:T(8,128)(2,1)S(1)} %get-tuple-element.107), kind=kOutput, calls=%fused_computation.65 | convolution fusion | flops 25165824 | bytes 2064384 | tf_op jit(solution)/shard_map/ihrk,hoikm->ohrm/dot_general | solution.py:101
  32.4 3.6 %collective-permute-done.6 = bf16[24,16,128]{2,1,0:T(8,128)(2,1)S(1)} collective-permute-done((bf16[24,16,128]{2,1,0:T(8,128)(2,1)S(1)}, bf16[24,16,128]{2,1,0:T(8,128)(2,1)S(1)}, u32[]{:S(2)}, u32[]{:S(2)}) %collective-permute-start.6) | collective-permute-done | bytes 98336 | tf_op jit(solution)/shard_map/ppermute | solution.py:26
  36.3 1.9 %fusion.57 = f32[2,24,16,128]{3,2,0,1:T(8,128)S(1)} fusion(bf16[4,24,2,2,64,128]{5,4,3,2,1,0:T(8,128)(2,1)} %param.21, bf16[2,24,16,64,1]{3,2,1,0,4:T(8,128)(2,1)S(1)} %get-tuple-element.104), kind=kOutput, calls=%fused_computation.66 | convolution fusion | flops 25165824 | bytes 2064384 | tf_op jit(solution)/shard_map/ihrk,hoikm->ohrm/dot_general | solution.py:98
  38.2 1.8 fusion.60
  41.3 3.8 %collective-permute-done.7 = bf16[24,16,128]{2,1,0:T(8,128)(2,1)S(1)} collective-permute-done((bf16[24,16,128]{2,1,0:T(8,128)(2,1)S(1)}, bf16[24,16,128]{2,1,0:T(8,128)(2,1)S(1)}, u32[]{:S(2)}, u32[]{:S(2)}) %collective-permute-start.7) | collective-permute-done | bytes 98336 | tf_op jit(solution)/shard_map/ppermute | solution.py:26
  46.6 1.3 fusion.89
  47.9 1.2 fusion.91
  49.1 1.2 pad_maximum_fusion.1
  50.4 126.6 %while.10 = (s32[]{:T(128)}, f32[48,2,16,128]{3,0,2,1:T(8,128)S(1)}, s32[]{:T(128)}, s32[144]{0:T(256)S(1)}, s32[144]{0:T(256)S(1)}, /*index=5*/bf16[144,2,16,12...) while((s32[]{:T(128)}, ...), condition=%wide.region_2.3_spmd, body=%wide.region_0.2_spmd.sunk | while | flops 49757228 | bytes 6537723 | solution.py:91
  53.2 2.2 %multiply_convert_fusion.4 = (bf16[8,128,128]{2,1,0:T(8,128)(2,1)S(1)}, bf16[8,128,128]{2,1,0:T(8,128)(2,1)S(1)}) fusion(f32[8,128,128]{2,1,0:T(8,128)S(1)} %multiply_reduce_fusion.2), kind=kLoop, calls=%fused_computation.16.clone.1 | loop fusion | flops 1048576 | bytes 1048576 | tf_op jit(solution)/shard_map/convert.2
  60.2 2.2 %multiply_convert_fusion.4 = (bf16[8,128,128]{2,1,0:T(8,128)(2,1)S(1)}, bf16[8,128,128]{2,1,0:T(8,128)(2,1)S(1)}) fusion(f32[8,128,128]{2,1,0:T(8,128)S(1)} %multiply_reduce_fusion.2), kind=kLoop, calls=%fused_computation.16.clone.1 | loop fusion | flops 1048576 | bytes 1048576 | tf_op jit(solution)/shard_map/convert.2
  65.6 1.1 fusion.144
  67.2 2.2 %multiply_convert_fusion.4 = (bf16[8,128,128]{2,1,0:T(8,128)(2,1)S(1)}, bf16[8,128,128]{2,1,0:T(8,128)(2,1)S(1)}) fusion(f32[8,128,128]{2,1,0:T(8,128)S(1)} %multiply_reduce_fusion.2), kind=kLoop, calls=%fused_computation.16.clone.1 | loop fusion | flops 1048576 | bytes 1048576 | tf_op jit(solution)/shard_map/convert.2
  74.2 2.2 %multiply_convert_fusion.4 = (bf16[8,128,128]{2,1,0:T(8,128)(2,1)S(1)}, bf16[8,128,128]{2,1,0:T(8,128)(2,1)S(1)}) fusion(f32[8,128,128]{2,1,0:T(8,128)S(1)} %multiply_reduce_fusion.2), kind=kLoop, calls=%fused_computation.16.clone.1 | loop fusion | flops 1048576 | bytes 1048576 | tf_op jit(solution)/shard_map/convert.2
  79.7 1.1 fusion.144
  81.3 2.2 %multiply_convert_fusion.4 = (bf16[8,128,128]{2,1,0:T(8,128)(2,1)S(1)}, bf16[8,128,128]{2,1,0:T(8,128)(2,1)S(1)}) fusion(f32[8,128,128]{2,1,0:T(8,128)S(1)} %multiply_reduce_fusion.2), kind=kLoop, calls=%fused_computation.16.clone.1 | loop fusion | flops 1048576 | bytes 1048576 | tf_op jit(solution)/shard_map/convert.2
  88.3 2.2 %multiply_convert_fusion.4 = (bf16[8,128,128]{2,1,0:T(8,128)(2,1)S(1)}, bf16[8,128,128]{2,1,0:T(8,128)(2,1)S(1)}) fusion(f32[8,128,128]{2,1,0:T(8,128)S(1)} %multiply_reduce_fusion.2), kind=kLoop, calls=%fused_computation.16.clone.1 | loop fusion | flops 1048576 | bytes 1048576 | tf_op jit(solution)/shard_map/convert.2
  95.3 2.2 %multiply_convert_fusion.4 = (bf16[8,128,128]{2,1,0:T(8,128)(2,1)S(1)}, bf16[8,128,128]{2,1,0:T(8,128)(2,1)S(1)}) fusion(f32[8,128,128]{2,1,0:T(8,128)S(1)} %multiply_reduce_fusion.2), kind=kLoop, calls=%fused_computation.16.clone.1 | loop fusion | flops 1048576 | bytes 1048576 | tf_op jit(solution)/shard_map/convert.2
  100.8 1.1 fusion.144
  102.4 2.2 %multiply_convert_fusion.4 = (bf16[8,128,128]{2,1,0:T(8,128)(2,1)S(1)}, bf16[8,128,128]{2,1,0:T(8,128)(2,1)S(1)}) fusion(f32[8,128,128]{2,1,0:T(8,128)S(1)} %multiply_reduce_fusion.2), kind=kLoop, calls=%fused_computation.16.clone.1 | loop fusion | flops 1048576 | bytes 1048576 | tf_op jit(solution)/shard_map/convert.2
  107.8 1.1 fusion.144
  109.4 2.2 %multiply_convert_fusion.4 = (bf16[8,128,128]{2,1,0:T(8,128)(2,1)S(1)}, bf16[8,128,128]{2,1,0:T(8,128)(2,1)S(1)}) fusion(f32[8,128,128]{2,1,0:T(8,128)S(1)} %multiply_reduce_fusion.2), kind=kLoop, calls=%fused_computation.16.clone.1 | loop fusion | flops 1048576 | bytes 1048576 | tf_op jit(solution)/shard_map/convert.2
  114.9 1.1 fusion.144
  116.4 2.2 %multiply_convert_fusion.4 = (bf16[8,128,128]{2,1,0:T(8,128)(2,1)S(1)}, bf16[8,128,128]{2,1,0:T(8,128)(2,1)S(1)}) fusion(f32[8,128,128]{2,1,0:T(8,128)S(1)} %multiply_reduce_fusion.2), kind=kLoop, calls=%fused_computation.16.clone.1 | loop fusion | flops 1048576 | bytes 1048576 | tf_op jit(solution)/shard_map/convert.2
  123.5 2.2 %multiply_convert_fusion.4 = (bf16[8,128,128]{2,1,0:T(8,128)(2,1)S(1)}, bf16[8,128,128]{2,1,0:T(8,128)(2,1)S(1)}) fusion(f32[8,128,128]{2,1,0:T(8,128)S(1)} %multiply_reduce_fusion.2), kind=kLoop, calls=%fused_computation.16.clone.1 | loop fusion | flops 1048576 | bytes 1048576 | tf_op jit(solution)/shard_map/convert.2
  128.9 1.1 fusion.144
  130.5 2.2 %multiply_convert_fusion.4 = (bf16[8,128,128]{2,1,0:T(8,128)(2,1)S(1)}, bf16[8,128,128]{2,1,0:T(8,128)(2,1)S(1)}) fusion(f32[8,128,128]{2,1,0:T(8,128)S(1)} %multiply_reduce_fusion.2), kind=kLoop, calls=%fused_computation.16.clone.1 | loop fusion | flops 1048576 | bytes 1048576 | tf_op jit(solution)/shard_map/convert.2
  135.9 1.1 fusion.144
  137.5 2.2 %multiply_convert_fusion.4 = (bf16[8,128,128]{2,1,0:T(8,128)(2,1)S(1)}, bf16[8,128,128]{2,1,0:T(8,128)(2,1)S(1)}) fusion(f32[8,128,128]{2,1,0:T(8,128)S(1)} %multiply_reduce_fusion.2), kind=kLoop, calls=%fused_computation.16.clone.1 | loop fusion | flops 1048576 | bytes 1048576 | tf_op jit(solution)/shard_map/convert.2
  143.0 1.1 fusion.144
  144.6 2.2 %multiply_convert_fusion.4 = (bf16[8,128,128]{2,1,0:T(8,128)(2,1)S(1)}, bf16[8,128,128]{2,1,0:T(8,128)(2,1)S(1)}) fusion(f32[8,128,128]{2,1,0:T(8,128)S(1)} %multiply_reduce_fusion.2), kind=kLoop, calls=%fused_computation.16.clone.1 | loop fusion | flops 1048576 | bytes 1048576 | tf_op jit(solution)/shard_map/convert.2
  150.0 1.1 fusion.144
  151.6 2.2 %multiply_convert_fusion.4 = (bf16[8,128,128]{2,1,0:T(8,128)(2,1)S(1)}, bf16[8,128,128]{2,1,0:T(8,128)(2,1)S(1)}) fusion(f32[8,128,128]{2,1,0:T(8,128)S(1)} %multiply_reduce_fusion.2), kind=kLoop, calls=%fused_computation.16.clone.1 | loop fusion | flops 1048576 | bytes 1048576 | tf_op jit(solution)/shard_map/convert.2
  158.6 2.2 %multiply_convert_fusion.4 = (bf16[8,128,128]{2,1,0:T(8,128)(2,1)S(1)}, bf16[8,128,128]{2,1,0:T(8,128)(2,1)S(1)}) fusion(f32[8,128,128]{2,1,0:T(8,128)S(1)} %multiply_reduce_fusion.2), kind=kLoop, calls=%fused_computation.16.clone.1 | loop fusion | flops 1048576 | bytes 1048576 | tf_op jit(solution)/shard_map/convert.2
  165.7 2.2 %multiply_convert_fusion.4 = (bf16[8,128,128]{2,1,0:T(8,128)(2,1)S(1)}, bf16[8,128,128]{2,1,0:T(8,128)(2,1)S(1)}) fusion(f32[8,128,128]{2,1,0:T(8,128)S(1)} %multiply_reduce_fusion.2), kind=kLoop, calls=%fused_computation.16.clone.1 | loop fusion | flops 1048576 | bytes 1048576 | tf_op jit(solution)/shard_map/convert.2
  172.7 2.2 %multiply_convert_fusion.4 = (bf16[8,128,128]{2,1,0:T(8,128)(2,1)S(1)}, bf16[8,128,128]{2,1,0:T(8,128)(2,1)S(1)}) fusion(f32[8,128,128]{2,1,0:T(8,128)S(1)} %multiply_reduce_fusion.2), kind=kLoop, calls=%fused_computation.16.clone.1 | loop fusion | flops 1048576 | bytes 1048576 | tf_op jit(solution)/shard_map/convert.2
  177.0 1.5 fusion.75
  180.5 1.1 copy.99
  (304 shorter events, 86.9 us)
Async XLA Ops:
  0.0 46.6 %copy-start = (bf16[48,64,256]{2,1,0:T(8,128)(2,1)S(1)}, bf16[48,64,256]{2,1,0:T(8,128)(2,1)}, u32[]{:S(2)}) copy-start(bf16[48,64,256]{2,1,0:T(8,128)(2,1)} %param.20) | copy-start | bytes 4718596
  0.0 2.4 %copy-start.1 = (bf16[48,128,128]{2,1,0:T(8,128)(2,1)S(1)}, bf16[48,128,128]{2,1,0:T(8,128)(2,1)}, u32[]{:S(2)}) copy-start(bf16[48,128,128]{2,1,0:T(8,128)(2,1)} %param.19) | copy-start | bytes 4718596
  3.5 5.5 %collective-permute-start.4 = (bf16[24,16,128]{2,1,0:T(8,128)(2,1)S(1)}, bf16[24,16,128]{2,1,0:T(8,128)(2,1)S(1)}, u32[]{:S(2)}, u32[]{:S(2)}) collective-permute-start(bf16[24,16,128]{2,1,0:T(8,128)(2,1)S(1)} %get-tuple-element.78), channel_id=1, source_target_pairs={{0,8},{8,0},{1,9},{9,1},{2,10},{10,2},{3,11},{11,3},{4,12},{12,4},... | collective-permute-start | bytes 294920 | tf_op jit(solution)/shard_map/ppermute | solution.py:26
  3.5 45.6 %collective-permute-start = (bf16[48,2,16,128]{3,2,1,0:T(8,128)(2,1)S(1)}, bf16[48,2,16,128]{3,2,1,0:T(8,128)(2,1)}, u32[]{:S(2)}, u32[]{:S(2)}) collective-permute-start(bf16[48,2,16,128]{3,2,1,0:T(8,128)(2,1)S(1)} %bitcast.323), channel_id=1, source_target_pairs={{0,1},{1,2},{2,3},{3,4},{4,5},{5,6},{6,7},{7,8},{8,9},{9,10},{10,1... | collective-permute-start | bytes 1179656 | tf_op jit(solution)/shard_map/ppermute | solution.py:17
  7.7 41.4 %collective-permute-start.1 = (bf16[48,2,16,128]{3,2,1,0:T(8,128)(2,1)S(1)}, bf16[48,2,16,128]{3,2,1,0:T(8,128)(2,1)}, u32[]{:S(2)}, u32[]{:S(2)}) collective-permute-start(bf16[48,2,16,128]{3,2,1,0:T(8,128)(2,1)S(1)} %bitcast.324), channel_id=1, source_target_pairs={{1,0},{2,1},{3,2},{4,3},{5,4},{6,5},{7,6},{8,7},{9,8},{10,9},{11,1... | collective-permute-start | bytes 1179656 | tf_op jit(solution)/shard_map/ppermute | solution.py:20
  12.9 4.4 %copy-start.3 = (bf16[48,3,128]{2,0,1:T(8,128)(2,1)S(1)}, bf16[48,3,128]{2,0,1:T(8,128)(2,1)}, u32[]{:S(2)}) copy-start(bf16[48,3,128]{2,0,1:T(8,128)(2,1)} %param.13) | copy-start | bytes 110596
  12.9 4.4 %copy-start.4 = (s32[1,48]{1,0:T(1,128)S(1)}, s32[1,48]{1,0:T(1,128)}, u32[]{:S(2)}) copy-start(s32[1,48]{1,0:T(1,128)} %param.15) | copy-start | bytes 580
  12.9 8.5 %copy-start.5 = (s32[16]{0:T(128)S(1)}, s32[16]{0:T(128)}, u32[]{:S(2)}) copy-start(s32[16]{0:T(128)} %param.18) | copy-start | bytes 196
  13.3 13.1 %collective-permute-start.5 = (bf16[24,16,128]{2,1,0:T(8,128)(2,1)S(1)}, bf16[24,16,128]{2,1,0:T(8,128)(2,1)S(1)}, u32[]{:S(2)}, u32[]{:S(2)}) collective-permute-start(bf16[24,16,128]{2,1,0:T(8,128)(2,1)S(1)} %get-tuple-element.76), channel_id=1, source_target_pairs={{0,4},{1,5},{2,6},{3,7},{4,0},{5,1},{6,2},{7,3},{8,12},{9,13},{10,... | collective-permute-start | bytes 294920 | tf_op jit(solution)/shard_map/ppermute | solution.py:26
  17.5 11.0 %copy-start.2 = (bf16[48,384]{1,0:T(8,128)(2,1)}, bf16[48,384]{1,0:T(8,128)(2,1)S(1)}, u32[]{:S(2)}) copy-start(bf16[48,384]{1,0:T(8,128)(2,1)S(1)} %convolution_convert_fusion.4) | copy-start | bytes 110596
  17.5 23.0 %collective-permute-start.2 = (bf16[48,3,128]{2,1,0:T(4,128)(2,1)S(1)}, bf16[48,3,128]{2,1,0:T(4,128)(2,1)S(1)}, u32[]{:S(2)}, u32[]{:S(2)}) collective-permute-start(bf16[48,3,128]{2,1,0:T(4,128)(2,1)S(1)} %reshape.91), channel_id=1, source_target_pairs={{0,1},{1,2},{2,3},{3,4},{4,5},{5,6},{6,7},{7,8},{8,9},{9,10},{10,1... | collective-permute-start | bytes 110600 | tf_op jit(solution)/shard_map/ppermute | solution.py:17
  20.1 20.4 %collective-permute-start.3 = (bf16[48,3,128]{2,1,0:T(4,128)(2,1)S(1)}, bf16[48,3,128]{2,1,0:T(4,128)(2,1)S(1)}, u32[]{:S(2)}, u32[]{:S(2)}) collective-permute-start(bf16[48,3,128]{2,1,0:T(4,128)(2,1)S(1)} %reshape.91), channel_id=1, source_target_pairs={{1,0},{2,1},{3,2},{4,3},{5,4},{6,5},{7,6},{8,7},{9,8},{10,9},{11,1... | collective-permute-start | bytes 110600 | tf_op jit(solution)/shard_map/ppermute | solution.py:20
  28.5 16.9 %slice-start = ((s8[6291456]{0:T(1024)(128)(4,1)}), s8[4194304]{0:T(1024)(128)(4,1)S(1)}, s32[]{:S(2)}) async-start(s8[6291456]{0:T(1024)(128)(4,1)} %bitcast.317), calls=%async_computation | async-start | bytes 8388608
  30.8 5.1 %collective-permute-start.6 = (bf16[24,16,128]{2,1,0:T(8,128)(2,1)S(1)}, bf16[24,16,128]{2,1,0:T(8,128)(2,1)S(1)}, u32[]{:S(2)}, u32[]{:S(2)}) collective-permute-start(bf16[24,16,128]{2,1,0:T(8,128)(2,1)S(1)} %get-tuple-element.74), channel_id=1, source_target_pairs={{0,2},{1,3},{2,0},{3,1},{4,6},{5,7},{6,4},{7,5},{8,10},{9,11},{10,... | collective-permute-start | bytes 294920 | tf_op jit(solution)/shard_map/ppermute | solution.py:26
  36.3 9.1 %slice-start.1 = ((s8[6291456]{0:T(1024)(128)(4,1)}), s8[2097152]{0:T(1024)(128)(4,1)S(1)}, s32[]{:S(2)}) async-start(s8[6291456]{0:T(1024)(128)(4,1)} %bitcast.317), calls=%async_computation.1 | async-start | bytes 4194304
  40.4 4.7 %collective-permute-start.7 = (bf16[24,16,128]{2,1,0:T(8,128)(2,1)S(1)}, bf16[24,16,128]{2,1,0:T(8,128)(2,1)S(1)}, u32[]{:S(2)}, u32[]{:S(2)}) collective-permute-start(bf16[24,16,128]{2,1,0:T(8,128)(2,1)S(1)} %get-tuple-element.72), channel_id=1, source_target_pairs={{0,1},{1,0},{2,3},{3,2},{4,5},{5,4},{6,7},{7,6},{8,9},{9,8},{10,11... | collective-permute-start | bytes 294920 | tf_op jit(solution)/shard_map/ppermute | solution.py:26
where the time goes:
time: 183 us; the launch traced here: 182 us
  matrix products  77.9 us (43%)
  other arithmetic  69.4 us (38%)
  starting transfers between devices  14.2 us (8%)
  waiting for transfers between devices  11.2 us (6%)
  local copies, waits for them, and re-layouts  6.31 us (3%)
    dot_general x56, matrix products, select_rows(): jnp.dot(selector, flat_table, preferred_element_type=jnp.float32)  45.6 us
    another operation x22, other arithmetic  40.3 us
    dot_general x19, matrix products, place_rows(): jnp.dot(selector.T, flat_values, preferred_element_type=jnp.float32, prec...  13.9 us
    convert_element_type x18, other arithmetic, step(): ((slot_ids >= lower_slot) & (slot_ids < upper_slot)).astype(jnp.float32)  11.3 us
    ppermute x4, waiting for transfers between devices, partner(): lax.ppermute(x, axis, [(i, i ^ 1 << stride) for i in range(lax.axis_size(...  11.2 us
    reduce_sum x18, other arithmetic, pair_kernels(): jnp.sum(offsets * offsets, axis=1) + softening * softening  8.57 us
    ppermute x2, starting transfers between devices, padded(): lax.ppermute(lax.slice_in_dim(block, block.shape[dim] - width, None, axis...  6.7 us
    dot_general x4, matrix products, butterfly_mix(): jnp.einsum('ihrk,hoikm->ohrm', stacked[..., rank_width:], weights, prefer...  5.87 us
  transfers between devices with their start and end apart: 8, of which 3 were waited for; matrix products, arithmetic and copies ran while one was open for 11% of the time, Pallas kernels for 0%

commit v1 on v0

v1 whole, which is shorter than its diff:
```python
import functools
import math

import jax
import jax.numpy as jnp
from jax import lax
from jax.experimental import pallas as pl
from jax.experimental.pallas import tpu as pltpu
from jax.sharding import PartitionSpec as P

wavenumber = 6.0
softening = 0.05

SIN = (3.14159264, -5.16771008, 2.55007752, -0.59829129, 0.07765766)
COS = (0.99999995, -4.93479283, 4.05841135, -1.33187657, 0.21968961)
PER_TURN = wavenumber / (2.0 * math.pi)
AMPLITUDE = PER_TURN / (4.0 * math.pi)
FEATURES = 16


def loop(count, body, width):
    width = math.gcd(count, width)

    def step(index, carry):
        for inner in range(width):
            body(index * width + inner)
        return carry

    lax.fori_loop(0, count // width, step, 0)


def poly(values, coeffs):
    total = coeffs[-1]
    for coeff in coeffs[-2::-1]:
        total = total * values + coeff
    return total


def pieces(values):
    parts = []
    for _ in range(3):
        part = values.astype(jnp.bfloat16).astype(jnp.float32)
        parts.append(part)
        values = values - part
    return parts


def kernel(
    ids,
    field,
    weight,
    positions,
    compress_hbm,
    expand_hbm,
    mixing_hbm,
    out,
    compress,
    expand,
    mixing,
    win,
    pts_raw,
    pts,
    src_feat,
    tgt_feat,
    tiles,
    coeffs,
    landed,
    far,
    running,
    load_sem,
    send_sem,
    recv_sem,
    *,
    pairs,
    spread,
    devices,
):
    panels = field.shape[0]
    rows = field.shape[1]
    half_rows = rows // 2
    width = field.shape[2]
    half = panels // 2
    levels = mixing.shape[0]
    rank2 = compress.shape[2]
    rank = rank2 // 2
    at_src, at_tgt, at_keep = 0, pairs, 2 * pairs
    at_order = 3 * pairs
    at_inv, at_end = at_order + panels, at_order + 2 * panels

    group = lax.axis_index("grp")
    slot = lax.axis_index("pan")
    device = group * spread + slot
    has_prev = device > 0
    has_next = device < devices - 1
    prev = lax.rem(device + devices - 1, devices)
    next_ = lax.rem(device + 1, devices)

    def place(number):
        return {"grp": number // spread, "pan": lax.rem(number, spread)}

    loads = [
        pltpu.make_async_copy(compress_hbm, compress, load_sem.at[0]),
        pltpu.make_async_copy(expand_hbm, expand, load_sem.at[1]),
    ] + [
        pltpu.make_async_copy(mixing_hbm.at[level], mixing.at[level], load_sem.at[2 + level])
        for level in range(levels)
    ]
    for load in loads:
        load.start()

    top_bit = spread.bit_length() - 1
    bits, partners = [], []
    for level in range(levels):
        if level == 0:
            bit = group
            partners.append({"grp": 1 - group, "pan": slot})
        else:
            stride = 1 << (top_bit - level)
            bit = lax.rem(slot // stride, 2)
            partners.append({"grp": group, "pan": slot + stride - 2 * stride * bit})
        bits.append(bit)

    barrier = pltpu.get_barrier_semaphore()
    for other in partners:
        pl.semaphore_signal(barrier, inc=1, device_id=other, device_id_type=pl.DeviceIdType.MESH)

    @pl.when(has_prev)
    def _():
        pl.semaphore_signal(
            barrier, inc=1, device_id=place(prev), device_id_type=pl.DeviceIdType.MESH
        )

    @pl.when(has_next)
    def _():
        pl.semaphore_signal(
            barrier, inc=1, device_id=place(next_), device_id_type=pl.DeviceIdType.MESH
        )

    def gather_points(panel):
        xyz = positions[ids[at_order + panel]].astype(jnp.float32)
        for axis in range(3):
            pts_raw[pl.ds(axis * panels + panel, 1), :] = xyz[axis : axis + 1, :]

    loop(panels, gather_points, 8)
    pts[3 * panels : 6 * panels] = pts_raw[...].astype(jnp.bfloat16)

    def third(ref, window):
        return ref.at[pl.ds(window * (ref.shape[0] // 3), ref.shape[0] // 3)]

    def window_copies(ref, base):
        to_next = pltpu.make_async_remote_copy(
            src_ref=third(ref, 1),
            dst_ref=third(ref, 0),
            send_sem=send_sem.at[base],
            recv_sem=recv_sem.at[base],
            device_id=place(next_),
            device_id_type=pl.DeviceIdType.MESH,
        )
        to_prev = pltpu.make_async_remote_copy(
            src_ref=third(ref, 1),
            dst_ref=third(ref, 2),
            send_sem=send_sem.at[base + 1],
            recv_sem=recv_sem.at[base + 1],
            device_id=place(prev),
            device_id_type=pl.DeviceIdType.MESH,
        )
        return to_next, to_prev

    def start_window(copies):
        @pl.when(has_next)
        def _():
            copies[0].start()

        @pl.when(has_prev)
        def _():
            copies[1].start()

    def wait_window(copies, ref):
        @pl.when(has_prev)
        def _():
            copies[0].wait_recv()
            copies[1].wait_send()

        @pl.when(has_next)
        def _():
            copies[1].wait_recv()
            copies[0].wait_send()

        @pl.when(jnp.logical_not(has_prev))
        def _():
            third(ref, 0)[...] = jnp.zeros((ref.shape[0] // 3,) + ref.shape[1:], ref.dtype)

        @pl.when(jnp.logical_not(has_next))
        def _():
            third(ref, 2)[...] = jnp.zeros((ref.shape[0] // 3,) + ref.shape[1:], ref.dtype)

    pl.semaphore_wait(
        barrier, levels + has_prev.astype(jnp.int32) + has_next.astype(jnp.int32)
    )
    point_copies = window_copies(pts, 0)
    start_window(point_copies)

    def gather_sources(panel):
        row = ids[at_order + panel]
        win[panels + panel] = (field[row] * weight[pl.ds(row, 1), :]).astype(jnp.bfloat16)

    loop(panels, gather_sources, 8)
    source_copies = window_copies(win, 2)

    lane = lax.broadcasted_iota(jnp.int32, (half_rows, rank2), 1)
    low_lanes = lane < rank
    sign = jnp.where(low_lanes, -1.0, 1.0)

    def fold(product):
        return product[:half_rows] + sign * pltpu.roll(product[half_rows:], rank, 1)

    loads[0].wait()

    def compress_panel(panel):
        product = jnp.dot(win[panels + panel], compress[panel], preferred_element_type=jnp.float32)
        coeffs[0, panel] = fold(product).astype(jnp.bfloat16)

    loop(panels, compress_panel, 8)

    def level_copy(level):
        return pltpu.make_async_remote_copy(
            src_ref=coeffs.at[level, pl.ds((1 - bits[level]) * half, half)],
            dst_ref=landed.at[level],
            send_sem=send_sem.at[4 + level],
            recv_sem=recv_sem.at[4 + level],
            device_id=partners[level],
            device_id_type=pl.DeviceIdType.MESH,
        )

    level_copies = [level_copy(0)]
    level_copies[0].start()
    start_window(source_copies)

    ones = jnp.ones((panels, width), jnp.float32)

    def source_features(window):
        xyz = third(pts, window)[...].astype(jnp.float32)
        square = jnp.full((panels, width), softening * softening, jnp.float32)
        stack = []
        for axis in range(3):
            x = xyz[axis * panels : (axis + 1) * panels]
            square = square + x * x
            stack += [x] * 3
        stack += pieces(square * (PER_TURN * PER_TURN)) + [ones] * 3 + [ones * 0.0]
        for row, values in enumerate(stack):
            src_feat[pl.ds(window * panels, panels), row, :] = values

    def target_features():
        xyz = third(pts, 1)[...].astype(jnp.float32)
        square = jnp.zeros((panels, width), jnp.float32)
        stack = []
        for axis in range(3):
            x = xyz[axis * panels : (axis + 1) * panels]
            square = square + x * x
            stack += pieces(x * (-2.0 * PER_TURN * PER_TURN))
        stack += [ones] * 3 + pieces(square * (PER_TURN * PER_TURN)) + [ones * 0.0]
        for row, values in enumerate(stack):
            tgt_feat[:, row, :] = values

    target_features()
    source_features(1)
    wait_window(point_copies, pts)
    source_features(0)
    source_features(2)

    def make_tile(pair):
        source = src_feat[ids[at_src + pair]].astype(jnp.bfloat16)
        target = tgt_feat[ids[at_tgt + pair]].astype(jnp.bfloat16)
        squared = lax.dot_general(
            source, target, (((0,), (0,)), ((), ())), preferred_element_type=jnp.float32
        )
        inverse = lax.rsqrt(squared)
        turns = squared * inverse
        part = turns - jnp.round(turns)
        square = part * part
        half_sin = part * poly(square, [math.sqrt(2.0 * AMPLITUDE) * c for c in SIN])
        half_cos = poly(square, [math.sqrt(2.0 * AMPLITUDE) * c for c in COS])
        scaled = inverse * half_sin
        tiles[pair, :, :width] = (AMPLITUDE * inverse - scaled * half_sin).astype(jnp.bfloat16)
        tiles[pair, :, width:] = (scaled * half_cos).astype(jnp.bfloat16)

    share = pairs // levels

    def mix_level(level):
        bit = bits[level]

        def mix_slot(index):
            kept = coeffs[level, bit * half + index].astype(jnp.float32)
            other = landed[level, index].astype(jnp.float32)
            low = jnp.where(bit == 1, other, kept)
            high = jnp.where(bit == 1, kept, other)
            real = jnp.where(low_lanes, low, pltpu.roll(high, rank, 1))
            imag = jnp.where(low_lanes, pltpu.roll(low, rank, 1), high)
            stacked = jnp.concatenate([real, imag], 0).astype(jnp.bfloat16)
            for side in range(2):
                product = jnp.dot(
                    stacked, mixing[level, index, side], preferred_element_type=jnp.float32
                )
                coeffs[level + 1, side * half + index] = fold(product).astype(jnp.bfloat16)

        loop(half, mix_slot, 8)

    for level in range(levels):
        first = level * share
        last = pairs if level == levels - 1 else first + share
        loop(last - first, lambda k, first=first: make_tile(first + k), 2)
        loads[2 + level].wait()
        level_copies[level].wait()
        mix_level(level)
        if level + 1 < levels:
            level_copies.append(level_copy(level + 1))
            level_copies[level + 1].start()

    loads[1].wait()

    def expand_panel(panel):
        values = coeffs[levels, panel].astype(jnp.float32)
        stacked = jnp.concatenate([values, pltpu.roll(values, rank, 1)], 0)[:, :rank]
        far[panel] = jnp.dot(
            stacked.astype(jnp.bfloat16), expand[panel], preferred_element_type=jnp.float32
        )

    loop(panels, expand_panel, 8)

    wait_window(source_copies, win)

    running[0] = jnp.zeros(running.shape[1:], jnp.float32)
    group_size = math.gcd(pairs, 4)

    def sum_pairs(index, total):
        for inner in range(group_size):
            pair = index * group_size + inner
            product = jnp.dot(
                win[ids[at_src + pair]],
                tiles[pair],
                preferred_element_type=jnp.float32,
            )
            total = total * ids[at_keep + pair].astype(jnp.float32) + product
            running[1 + pair] = total
        return total

    lax.fori_loop(
        0, pairs // group_size, sum_pairs, jnp.zeros(running.shape[1:], jnp.float32)
    )

    def write_panel(panel):
        total = far[ids[at_inv + panel]] + running[ids[at_end + panel]]
        out[panel, :half_rows] = total[:half_rows, :width] - total[half_rows:, width:]
        out[panel, half_rows:] = total[:half_rows, width:] + total[half_rows:, :width]

    loop(panels, write_panel, 8)


def pair_ids(order, target, source, count):
    panels, pairs = order.shape[0], target.shape[0]
    slots = jnp.arange(pairs, dtype=jnp.int32)
    target = jnp.where(slots < count, target, panels)
    key = target * pairs + slots
    rank = jnp.sum((key[None, :] < key[:, None]).astype(jnp.int32), 1)
    hit = rank[None, :] == slots[:, None]
    both = jnp.sum(jnp.where(hit, (target * (4 * panels) + source)[None, :], 0), 1)
    by_target, by_source = both // (4 * panels), both % (4 * panels)
    keep = jnp.concatenate(
        [jnp.zeros((1,), jnp.int32), (by_target[1:] == by_target[:-1]).astype(jnp.int32)]
    )
    rows = jnp.arange(panels, dtype=jnp.int32)
    inverse = jnp.sum(jnp.where(order[None, :] == rows[:, None], rows[None, :], 0), 1)
    up_to = jnp.sum((target[None, :] <= inverse[:, None]).astype(jnp.int32), 1)
    own = jnp.any(target[None, :] == inverse[:, None], 1)
    end = jnp.where(own, up_to, 0)
    return jnp.concatenate(
        [by_source, jnp.minimum(by_target, panels - 1), keep, order, inverse, end]
    )


def on_device(
    surface_field,
    positions,
    quad_weight,
    octree_order,
    near_target,
    near_source,
    near_count,
    compress,
    expand,
    mixing,
):
    panels, _, rhs, width = surface_field.shape
    levels, half = mixing.shape[:2]
    pairs = near_target.shape[1]
    rank2 = compress.shape[2]
    spread = lax.axis_size("pan")
    devices = spread * lax.axis_size("grp")
    device = lax.axis_index("grp") * spread + lax.axis_index("pan")
    ids = pair_ids(octree_order[0], near_target[device], near_source[device], near_count[device])
    rows = 2 * rhs
    vmem = pl.BlockSpec(memory_space=pltpu.VMEM)
    hbm = pl.BlockSpec(memory_space=pl.ANY)
    result = pl.pallas_call(
        functools.partial(kernel, pairs=pairs, spread=spread, devices=devices),
        out_shape=jax.ShapeDtypeStruct((panels, rows, width), jnp.float32),
        in_specs=[pl.BlockSpec(memory_space=pltpu.SMEM), vmem, vmem, vmem, hbm, hbm, hbm],
        out_specs=vmem,
        scratch_shapes=[
            pltpu.VMEM(compress.shape, jnp.bfloat16),
            pltpu.VMEM(expand.shape, jnp.bfloat16),
            pltpu.VMEM((levels, half, 2, rank2, rank2), jnp.bfloat16),
            pltpu.VMEM((3 * panels, rows, width), jnp.bfloat16),
            pltpu.VMEM((3 * panels, width), jnp.float32),
            pltpu.VMEM((9 * panels, width), jnp.bfloat16),
            pltpu.VMEM((3 * panels, FEATURES, width), jnp.float32),
            pltpu.VMEM((panels, FEATURES, width), jnp.float32),
            pltpu.VMEM((pairs, width, 2 * width), jnp.bfloat16),
            pltpu.VMEM((levels + 1, panels, rhs, rank2), jnp.bfloat16),
            pltpu.VMEM((levels, half, rhs, rank2), jnp.bfloat16),
            pltpu.VMEM((panels, rows, 2 * width), jnp.float32),
            pltpu.VMEM((pairs + 1, rows, 2 * width), jnp.float32),
            pltpu.SemaphoreType.DMA((2 + levels,)),
            pltpu.SemaphoreType.DMA((4 + levels,)),
            pltpu.SemaphoreType.DMA((4 + levels,)),
        ],
        compiler_params=pltpu.CompilerParams(
            collective_id=0, has_side_effects=True, vmem_limit_bytes=56 * 1024 * 1024
        ),
    )(
        ids,
        surface_field.reshape(panels, rows, width),
        quad_weight,
        positions,
        compress,
        expand,
        mixing.reshape(levels, half, 2, rank2, rank2),
    )
    return result.reshape(panels, 2, rhs, width)


def solution(mesh):
    placed = (
        P(("parts", "grp", "pan"), None, None, None),
        P(("parts", "grp", "pan"), None, None),
        P(("parts", "grp", "pan"), None),
        P(("parts", "grp", "pan"), None),
        P("parts", None),
        P("parts", None),
        P("parts"),
        P(("parts", "grp", "pan"), None, None),
        P(("parts", "grp", "pan"), None, None),
        P(None, ("parts", "grp", "pan"), None, None, None, None),
    )
    return jax.shard_map(
        on_device,
        mesh=mesh,
        in_specs=placed,
        out_specs=P(("parts", "grp", "pan"), None, None, None),
        check_vma=False,
    )
```

time: 183 us -> 83.8 us (0.46)
  the two profiles are of different devices: /device:TPU:2 before, /device:TPU:1 now
where the time goes in v1:
time: 83.8 us; the launch traced here: 83.2 us
  Pallas kernels  72.8 us (87%)
  local copies, waits for them, and re-layouts  6.03 us (7%)
  other arithmetic  4.25 us (5%)
    pallas_call x1, Pallas kernels, on_device(): pl.pallas_call(functools.partial(kernel, pairs=pairs, spread=spread, devi...  72.8 us
    unnamed x2, local copies, waits for them, and re-layouts  3.47 us
    add x2, other arithmetic, pair_ids(): key = target * pairs + slots  2.01 us

profile of v1, /device:TPU:1, one launch (start us, length us, event | category | flops | bytes accessed | tf_op | source)
XLA Modules:
  0.0 83.2 jit_solution(14462988359404966870)
XLA Ops:
  0.0 1.2 %dynamic_slice.9 = s32[1]{0:T(128)} dynamic-slice(s32[16]{0:T(128)} %param.16, s32[]{:T(128)S(6)} %select_n.42), dynamic_slice_sizes={1} | dynamic-slice | bytes 12 | tf_op jit(solution)/shard_map/dynamic_slice | solution.py:400
  1.2 0.8 select_reduce_fusion.1
  2.0 1.4 %iota_add_fusion = (s32[1,144]{1,0:T(1,128)S(1)}, s32[1,144]{1,0:T(1,128)S(1)}, s32[1,144]{1,0:T(1,128)S(1)}) fusion(s32[]{:T(128)} %bitcast, s32[16,144]{1,0:T(8,128)} %param.14, s32[]{:T(128)S(6)} %select_n.42), kind=kLoop, calls=%fused_computation.15 | loop fusion | flops 576 | bytes 2312 | tf_op jit(solution)/shard_map/add | solution.py:363
  3.4 0.6 fusion.1
  4.0 0.2 convert_reduce_fusion
  4.2 0.2 convert_reduce_fusion.1
  4.4 0.2 compare_reduce_fusion
  4.6 0.7 dynamic-slice_add_fusion
  5.3 0.1 select_reduce_fusion
  5.4 0.1 compare_convert_fusion
  5.5 1.3 %concatenate.3.ids = s32[576]{0:T(1024)} concatenate(s32[144]{0:T(256)S(1)} %get-tuple-element.10, s32[144]{0:T(256)S(1)} %get-tuple-element.5, s32[1]{0:T(128)} %constant.43.clone.1, s32[143]{0:T(256)S(1)} %compare_convert_fusion, s32[48]{0:T(128)} %bitcast.18, s32[48]{0:T(128)S(1)} %select_reduce_fusion.1, s32[48]{0:T(128)S(1)} %broadcast_select_fusion), dimensions={0} | concatenate | bytes 4608 | tf_op jit(solution)/shard_map/concatenate | solution.py:376
  6.8 1.4 %copy.12.positions = bf16[48,3,128]{2,1,0:T(4,128)(2,1)} copy(bf16[48,3,128]{2,0,1:T(8,128)(2,1)} %param.11) | data formatting | bytes 73728 | tf_op args[1]
  8.2 72.8 %shard_map.100 = f32[48,32,128]{2,1,0:T(8,128)} custom-call(s32[576]{0:T(1024)} %concatenate.3.ids, f32[48,32,128]{2,1,0:T(8,128)} %bitcast.11, f32[48,128]{1,0:T(8,128)} %weight.1, bf16[48,3,128]{2,1,0:T(4,128)(2,1)} %copy.12.positions, bf16[48,128,128]{2,1,0:T(8,128)(2,1)} %compress_hbm.1, bf16[48,64,256]{2,1,0:T(8,128)(2,1)} %expand_hbm.1, ...), custom_call_target="tpu_custom_call" | custom-call | tf_op jit(solution)/shard_map/pallas_call | solution.py:404
  81.1 2.1 %copy.14 = f32[48,2,16,128]{3,2,1,0:T(8,128)} copy(f32[48,2,16,128]{3,2,1,0:T(8,128)} %bitcast.10) | data formatting | bytes 1572864
  (2 shorter events, 0.0 us)

commit v2 on v1

--- a/solution.py
+++ b/solution.py
@@ -18,12 +18,15 @@
 FEATURES = 16
 
 
-def loop(count, body, width):
+def loop(count, load, compute, store, width):
     width = math.gcd(count, width)
 
     def step(index, carry):
-        for inner in range(width):
-            body(index * width + inner)
+        numbers = [index * width + inner for inner in range(width)]
+        values = [load(number) for number in numbers]
+        results = [compute(*value) for value in values]
+        for number, result in zip(numbers, results):
+            store(number, result)
         return carry
 
     lax.fori_loop(0, count // width, step, 0)
@@ -46,18 +49,31 @@
 
 
 def kernel(
-    ids,
+    order_hbm,
+    near_target_hbm,
+    near_source_hbm,
+    near_count_hbm,
+    field_hbm,
+    weight_hbm,
+    positions_hbm,
+    compress_hbm,
+    expand_hbm,
+    mixing_hbm,
+    out_hbm,
+    order,
+    order_vec,
+    near_target,
+    near_source,
+    near_count,
     field,
     weight,
     positions,
-    compress_hbm,
-    expand_hbm,
-    mixing_hbm,
     out,
     compress,
     expand,
     mixing,
     win,
+    pts_input,
     pts_raw,
     pts,
     src_feat,
@@ -67,6 +83,8 @@
     landed,
     far,
     running,
+    ids_vec,
+    ids,
     load_sem,
     send_sem,
     recv_sem,
@@ -83,9 +101,6 @@
     levels = mixing.shape[0]
     rank2 = compress.shape[2]
     rank = rank2 // 2
-    at_src, at_tgt, at_keep = 0, pairs, 2 * pairs
-    at_order = 3 * pairs
-    at_inv, at_end = at_order + panels, at_order + 2 * panels
 
     group = lax.axis_index("grp")
     slot = lax.axis_index("pan")
@@ -95,6 +110,14 @@
     prev = lax.rem(device + devices - 1, devices)
     next_ = lax.rem(device + 1, devices)
 
+    odd = lax.rem(device, 2)
+    has_before, has_after = device > 1, device < devices - 2
+    before = lax.rem(device + devices - 2, devices)
+    after = lax.rem(device + 2, devices)
+    passes = jnp.where(odd == 1, device - 2 >= 0, device + 2 < devices)
+    gets = jnp.where(odd == 1, device + 2 < devices, device - 2 >= 0)
+    pass_to = jnp.where(odd == 1, before, after)
+
     def place(number):
         return {"grp": number // spread, "pan": lax.rem(number, spread)}
 
@@ -105,7 +128,22 @@
         pltpu.make_async_copy(mixing_hbm.at[level], mixing.at[level], load_sem.at[2 + level])
         for level in range(levels)
     ]
-    for load in loads:
+    small = [
+        pltpu.make_async_copy(source, target, load_sem.at[3 + levels + number])
+        for number, (source, target) in enumerate(
+            [
+                (order_hbm, order),
+                (positions_hbm, positions),
+                (weight_hbm, weight),
+                (field_hbm, field),
+                (order_hbm, order_vec),
+                (near_target_hbm, near_target),
+                (near_source_hbm, near_source),
+                (near_count_hbm, near_count),
+            ]
+        )
+    ]
+    for load in small + loads:
         load.start()
 
     top_bit = spread.bit_length() - 1
@@ -136,12 +174,19 @@
             barrier, inc=1, device_id=place(next_), device_id_type=pl.DeviceIdType.MESH
         )
 
-    def gather_points(panel):
-        xyz = positions[ids[at_order + panel]].astype(jnp.float32)
+    small[0].wait()
+    small[1].wait()
+    pts_input[...] = positions[...].astype(jnp.float32)
+
+    def load_panel(panel):
+        row = order[0, panel]
+        return [pts_input[pl.ds(axis * panels + row, 1), :] for axis in range(3)]
+
+    def store_panel(panel, xyz):
         for axis in range(3):
-            pts_raw[pl.ds(axis * panels + panel, 1), :] = xyz[axis : axis + 1, :]
-
-    loop(panels, gather_points, 8)
+            pts_raw[pl.ds(axis * panels + panel, 1), :] = xyz[axis]
+
+    loop(panels, load_panel, lambda *xyz: xyz, store_panel, 16)
     pts[3 * panels : 6 * panels] = pts_raw[...].astype(jnp.bfloat16)
 
     def third(ref, window):
@@ -194,18 +239,54 @@
         def _():
             third(ref, 2)[...] = jnp.zeros((ref.shape[0] // 3,) + ref.shape[1:], ref.dtype)
 
+    for reached, target in ((has_before, before), (has_after, after)):
+
+        @pl.when(reached)
+        def _(target=target):
+            pl.semaphore_signal(
+                barrier, inc=1, device_id=place(target), device_id_type=pl.DeviceIdType.MESH
+            )
+
     pl.semaphore_wait(
-        barrier, levels + has_prev.astype(jnp.int32) + has_next.astype(jnp.int32)
+        barrier,
+        levels + sum(reached.astype(jnp.int32) for reached in (has_prev, has_next, has_before, has_after)),
     )
     point_copies = window_copies(pts, 0)
     start_window(point_copies)
 
-    def gather_sources(panel):
-        row = ids[at_order + panel]
-        win[panels + panel] = (field[row] * weight[pl.ds(row, 1), :]).astype(jnp.bfloat16)
-
-    loop(panels, gather_sources, 8)
-    source_copies = window_copies(win, 2)
+    def load_source(panel):
+        row = order[0, panel]
+        return field[row], weight[pl.ds(row, 1), :]
+
+    def store_source(panel, values):
+        win[panels + panel] = values
+
+    small[2].wait()
+    small[3].wait()
+    loop(panels, load_source, lambda x, w: (x * w).astype(jnp.bfloat16), store_source, 8)
+
+    chunk = panels // levels
+
+    def window_piece(third_from, third_to, piece, base, target):
+        return pltpu.make_async_remote_copy(
+            src_ref=win.at[pl.ds(third_from * panels + piece * chunk, chunk)],
+            dst_ref=win.at[pl.ds(third_to * panels + piece * chunk, chunk)],
+            send_sem=send_sem.at[base + piece],
+            recv_sem=recv_sem.at[base + piece],
+            device_id=place(target),
+            device_id_type=pl.DeviceIdType.MESH,
+        )
+
+    direct = [
+        window_piece(1, 2 * odd, piece, 4 + levels, device + 1 - 2 * odd)
+        for piece in range(levels)
+    ]
+    passed = [
+        window_piece(2 - 2 * odd, 2 * odd, piece, 4 + 2 * levels, pass_to)
+        for piece in range(levels)
+    ]
+    for copy in direct:
+        copy.start()
 
     lane = lax.broadcasted_iota(jnp.int32, (half_rows, rank2), 1)
     low_lanes = lane < rank
@@ -216,11 +297,19 @@
 
     loads[0].wait()
 
-    def compress_panel(panel):
-        product = jnp.dot(win[panels + panel], compress[panel], preferred_element_type=jnp.float32)
-        coeffs[0, panel] = fold(product).astype(jnp.bfloat16)
-
-    loop(panels, compress_panel, 8)
+    def matmul(left, right):
+        return jnp.dot(left, right, preferred_element_type=jnp.float32)
+
+    def store_compressed(panel, values):
+        coeffs[0, panel] = values
+
+    loop(
+        panels,
+        lambda panel: (win[panels + panel], compress[panel]),
+        lambda x, w: fold(matmul(x, w)).astype(jnp.bfloat16),
+        store_compressed,
+        16,
+    )
 
     def level_copy(level):
         return pltpu.make_async_remote_copy(
@@ -234,7 +323,6 @@
 
     level_copies = [level_copy(0)]
     level_copies[0].start()
-    start_window(source_copies)
 
     ones = jnp.ones((panels, width), jnp.float32)
 
@@ -262,17 +350,33 @@
         for row, values in enumerate(stack):
             tgt_feat[:, row, :] = values
 
+    for load in small[4:]:
+        load.wait()
+    sort_pairs(
+        order_vec[...],
+        near_target[pl.ds(device, 1), :],
+        near_source[pl.ds(device, 1), :],
+        near_count[device],
+        ids_vec,
+    )
+    ids_copy = pltpu.make_async_copy(ids_vec, ids, load_sem.at[2 + levels])
+    ids_copy.start()
     target_features()
     source_features(1)
+    ids_copy.wait()
     wait_window(point_copies, pts)
     source_features(0)
     source_features(2)
 
-    def make_tile(pair):
-        source = src_feat[ids[at_src + pair]].astype(jnp.bfloat16)
-        target = tgt_feat[ids[at_tgt + pair]].astype(jnp.bfloat16)
+    def load_points(pair):
+        return src_feat[ids[0, pair]], tgt_feat[ids[1, pair]]
+
+    def make_tile(source, target):
         squared = lax.dot_general(
-            source, target, (((0,), (0,)), ((), ())), preferred_element_type=jnp.float32
+            source.astype(jnp.bfloat16),
+            target.astype(jnp.bfloat16),
+            (((0,), (0,)), ((), ())),
+            preferred_element_type=jnp.float32,
         )
         inverse = lax.rsqrt(squared)
         turns = squared * inverse
@@ -281,34 +385,54 @@
         half_sin = part * poly(square, [math.sqrt(2.0 * AMPLITUDE) * c for c in SIN])
         half_cos = poly(square, [math.sqrt(2.0 * AMPLITUDE) * c for c in COS])
         scaled = inverse * half_sin
-        tiles[pair, :, :width] = (AMPLITUDE * inverse - scaled * half_sin).astype(jnp.bfloat16)
-        tiles[pair, :, width:] = (scaled * half_cos).astype(jnp.bfloat16)
+        real = AMPLITUDE * inverse - scaled * half_sin
+        return real.astype(jnp.bfloat16), (scaled * half_cos).astype(jnp.bfloat16)
 
     share = pairs // levels
 
     def mix_level(level):
         bit = bits[level]
 
-        def mix_slot(index):
-            kept = coeffs[level, bit * half + index].astype(jnp.float32)
-            other = landed[level, index].astype(jnp.float32)
+        def load_slot(index):
+            weights = [mixing[level, index, side] for side in range(2)]
+            return (coeffs[level, bit * half + index], landed[level, index], *weights)
+
+        def mix_slot(kept, other, *weights):
+            kept, other = kept.astype(jnp.float32), other.astype(jnp.float32)
             low = jnp.where(bit == 1, other, kept)
             high = jnp.where(bit == 1, kept, other)
             real = jnp.where(low_lanes, low, pltpu.roll(high, rank, 1))
             imag = jnp.where(low_lanes, pltpu.roll(low, rank, 1), high)
             stacked = jnp.concatenate([real, imag], 0).astype(jnp.bfloat16)
+            return [fold(matmul(stacked, w)).astype(jnp.bfloat16) for w in weights]
+
+        def store_slot(index, values):
             for side in range(2):
-                product = jnp.dot(
-                    stacked, mixing[level, index, side], preferred_element_type=jnp.float32
-                )
-                coeffs[level + 1, side * half + index] = fold(product).astype(jnp.bfloat16)
-
-        loop(half, mix_slot, 8)
+                coeffs[level + 1, side * half + index] = values[side]
+
+        loop(half, load_slot, mix_slot, store_slot, 24)
 
     for level in range(levels):
         first = level * share
         last = pairs if level == levels - 1 else first + share
-        loop(last - first, lambda k, first=first: make_tile(first + k), 2)
+
+        def store_tile(pair, values, first=first):
+            tiles[first + pair, :, :width] = values[0]
+            tiles[first + pair, :, width:] = values[1]
+
+        loop(
+            last - first,
+            lambda pair, first=first: load_points(first + pair),
+            make_tile,
+            store_tile,
+            6,
+        )
+        direct[level].wait_recv()
+
+        @pl.when(passes)
+        def _(level=level):
+            passed[level].start()
+
         loads[2 + level].wait()
         level_copies[level].wait()
         mix_level(level)
@@ -318,29 +442,47 @@
 
     loads[1].wait()
 
-    def expand_panel(panel):
-        values = coeffs[levels, panel].astype(jnp.float32)
+    def expand_panel(values, weights):
+        values = values.astype(jnp.float32)
         stacked = jnp.concatenate([values, pltpu.roll(values, rank, 1)], 0)[:, :rank]
-        far[panel] = jnp.dot(
-            stacked.astype(jnp.bfloat16), expand[panel], preferred_element_type=jnp.float32
-        )
-
-    loop(panels, expand_panel, 8)
-
-    wait_window(source_copies, win)
+        return matmul(stacked.astype(jnp.bfloat16), weights)
+
+    def store_far(panel, values):
+        far[panel] = values
+
+    loop(
+        panels,
+        lambda panel: (coeffs[levels, panel], expand[panel]),
+        expand_panel,
+        store_far,
+        16,
+    )
+
+    for copy in direct:
+        copy.wait_send()
+
+    @pl.when(passes)
+    def _():
+        for copy in passed:
+            copy.wait_send()
+
+    @pl.when(gets)
+    def _():
+        for copy in passed:
+            copy.wait_recv()
+
+    @pl.when(jnp.logical_not(gets))
+    def _():
+        win[pl.ds(2 * odd * panels, panels)] = jnp.zeros((panels, rows, width), win.dtype)
 
     running[0] = jnp.zeros(running.shape[1:], jnp.float32)
-    group_size = math.gcd(pairs, 4)
+    group_size = math.gcd(pairs, 16)
 
     def sum_pairs(index, total):
-        for inner in range(group_size):
-            pair = index * group_size + inner
-            product = jnp.dot(
-                win[ids[at_src + pair]],
-                tiles[pair],
-                preferred_element_type=jnp.float32,
-            )
-            total = total * ids[at_keep + pair].astype(jnp.float32) + product
+        numbers = [index * group_size + inner for inner in range(group_size)]
+        products = [matmul(win[ids[0, pair]], tiles[pair]) for pair in numbers]
+        for pair, product in zip(numbers, products):
+            total = total * ids[2, pair].astype(jnp.float32) + product
             running[1 + pair] = total
         return total
 
@@ -348,34 +490,67 @@
         0, pairs // group_size, sum_pairs, jnp.zeros(running.shape[1:], jnp.float32)
     )
 
-    def write_panel(panel):
-        total = far[ids[at_inv + panel]] + running[ids[at_end + panel]]
+    def write_panel(panel, total):
         out[panel, :half_rows] = total[:half_rows, :width] - total[half_rows:, width:]
         out[panel, half_rows:] = total[:half_rows, width:] + total[half_rows:, :width]
 
-    loop(panels, write_panel, 8)
-
-
-def pair_ids(order, target, source, count):
-    panels, pairs = order.shape[0], target.shape[0]
-    slots = jnp.arange(pairs, dtype=jnp.int32)
-    target = jnp.where(slots < count, target, panels)
-    key = target * pairs + slots
-    rank = jnp.sum((key[None, :] < key[:, None]).astype(jnp.int32), 1)
-    hit = rank[None, :] == slots[:, None]
-    both = jnp.sum(jnp.where(hit, (target * (4 * panels) + source)[None, :], 0), 1)
-    by_target, by_source = both // (4 * panels), both % (4 * panels)
-    keep = jnp.concatenate(
-        [jnp.zeros((1,), jnp.int32), (by_target[1:] == by_target[:-1]).astype(jnp.int32)]
-    )
-    rows = jnp.arange(panels, dtype=jnp.int32)
-    inverse = jnp.sum(jnp.where(order[None, :] == rows[:, None], rows[None, :], 0), 1)
-    up_to = jnp.sum((target[None, :] <= inverse[:, None]).astype(jnp.int32), 1)
-    own = jnp.any(target[None, :] == inverse[:, None], 1)
-    end = jnp.where(own, up_to, 0)
-    return jnp.concatenate(
-        [by_source, jnp.minimum(by_target, panels - 1), keep, order, inverse, end]
-    )
+    out_chunk = panels // levels
+    out_copies = []
+    for piece in range(levels):
+        first = piece * out_chunk
+        loop(
+            out_chunk,
+            lambda panel, first=first: (far[ids[3, first + panel]], running[ids[4, first + panel]]),
+            lambda x, y: x + y,
+            lambda panel, total, first=first: write_panel(first + panel, total),
+            6,
+        )
+        out_copies.append(
+            pltpu.make_async_copy(
+                out.at[pl.ds(first, out_chunk)],
+                out_hbm.at[pl.ds(first, out_chunk)],
+                load_sem.at[11 + levels + piece],
+            )
+        )
+        out_copies[-1].start()
+    for copy in out_copies:
+        copy.wait()
+
+
+def sort_pairs(order, target, source, count, ids_vec):
+    panels, pairs = order.shape[1], target.shape[1]
+
+    def square(size, axis):
+        return lax.broadcasted_iota(jnp.int32, (size, size), axis)
+
+    def column(row, size):
+        picked = jnp.where(square(size, 0) == square(size, 1), row, 0)
+        return jnp.sum(picked, 1, keepdims=True)
+
+    number = lax.broadcasted_iota(jnp.int32, (1, pairs), 1)
+    target = jnp.where(number < count, target, panels)
+    key = target * pairs + number
+    key_col, target_col = column(key, pairs), column(target, pairs)
+    source_col = column(source, pairs)
+    rank = jnp.sum((key < key_col).astype(jnp.int32), 1, keepdims=True)
+
+    def picked(shift, values):
+        hit = rank == square(pairs, 1) - shift
+        return jnp.sum(jnp.where(hit, values, 0), 0, keepdims=True)
+
+    by_target = picked(0, target_col)
+    ids_vec[0:1, :] = picked(0, source_col)
+    ids_vec[1:2, :] = jnp.minimum(by_target, panels - 1)
+    ids_vec[2:3, :] = (by_target == picked(1, target_col)).astype(jnp.int32)
+    order_col = column(order, panels)
+    inverse = jnp.sum(
+        jnp.where(order_col == square(panels, 1), square(panels, 0), 0), 0, keepdims=True
+    )
+    inverse = jnp.minimum(inverse, panels - 1)
+    up_to = jnp.sum((target_col <= inverse).astype(jnp.int32), 0, keepdims=True)
+    own = jnp.sum((target_col == inverse).astype(jnp.int32), 0, keepdims=True)
+    ids_vec[3:4, :panels] = inverse
+    ids_vec[4:5, :panels] = jnp.where(own > 0, up_to, 0)
 
 
 def on_device(
@@ -396,21 +571,28 @@
     rank2 = compress.shape[2]
     spread = lax.axis_size("pan")
     devices = spread * lax.axis_size("grp")
-    device = lax.axis_index("grp") * spread + lax.axis_index("pan")
-    ids = pair_ids(octree_order[0], near_target[device], near_source[device], near_count[device])
     rows = 2 * rhs
-    vmem = pl.BlockSpec(memory_space=pltpu.VMEM)
     hbm = pl.BlockSpec(memory_space=pl.ANY)
     result = pl.pallas_call(
         functools.partial(kernel, pairs=pairs, spread=spread, devices=devices),
         out_shape=jax.ShapeDtypeStruct((panels, rows, width), jnp.float32),
-        in_specs=[pl.BlockSpec(memory_space=pltpu.SMEM), vmem, vmem, vmem, hbm, hbm, hbm],
-        out_specs=vmem,
+        in_specs=[hbm] * 10,
+        out_specs=hbm,
         scratch_shapes=[
+            pltpu.SMEM(octree_order.shape, jnp.int32),
+            pltpu.VMEM(octree_order.shape, jnp.int32),
+            pltpu.VMEM(near_target.shape, jnp.int32),
+            pltpu.VMEM(near_source.shape, jnp.int32),
+            pltpu.SMEM(near_count.shape, jnp.int32),
+            pltpu.VMEM((panels, rows, width), jnp.float32),
+            pltpu.VMEM(quad_weight.shape, jnp.float32),
+            pltpu.VMEM((3 * panels, width), jnp.bfloat16),
+            pltpu.VMEM((panels, rows, width), jnp.float32),
             pltpu.VMEM(compress.shape, jnp.bfloat16),
             pltpu.VMEM(expand.shape, jnp.bfloat16),
             pltpu.VMEM((levels, half, 2, rank2, rank2), jnp.bfloat16),
             pltpu.VMEM((3 * panels, rows, width), jnp.bfloat16),
+            pltpu.VMEM((3 * panels, width), jnp.float32),
             pltpu.VMEM((3 * panels, width), jnp.float32),
             pltpu.VMEM((9 * panels, width), jnp.bfloat16),
             pltpu.VMEM((3 * panels, FEATURES, width), jnp.float32),
@@ -420,18 +602,23 @@
             pltpu.VMEM((levels, half, rhs, rank2), jnp.bfloat16),
             pltpu.VMEM((panels, rows, 2 * width), jnp.float32),
             pltpu.VMEM((pairs + 1, rows, 2 * width), jnp.float32),
-            pltpu.SemaphoreType.DMA((2 + levels,)),
-            pltpu.SemaphoreType.DMA((4 + levels,)),
-            pltpu.SemaphoreType.DMA((4 + levels,)),
+            pltpu.VMEM((8, pairs), jnp.int32),
+            pltpu.SMEM((8, pairs), jnp.int32),
+            pltpu.SemaphoreType.DMA((11 + 2 * levels,)),
+            pltpu.SemaphoreType.DMA((4 + 3 * levels,)),
+            pltpu.SemaphoreType.DMA((4 + 3 * levels,)),
         ],
         compiler_params=pltpu.CompilerParams(
             collective_id=0, has_side_effects=True, vmem_limit_bytes=56 * 1024 * 1024
         ),
     )(
-        ids,
+        octree_order,
+        near_target,
+        near_source,
+        near_count,
         surface_field.reshape(panels, rows, width),
         quad_weight,
-        positions,
+        positions.transpose(1, 0, 2).reshape(3 * panels, width),
         compress,
         expand,
         mixing.reshape(levels, half, 2, rank2, rank2),

time: 83.8 us -> 40.1 us (0.48)
  Pallas kernels: 72.8 us -> 37.9 us
  other arithmetic: 4.25 us -> 0 us
  local copies, waits for them, and re-layouts: 6.03 us -> 2.06 us
    pallas_call x1, Pallas kernels: 72.8 us -> 37.9 us  [on_device(): pl.pallas_call(functools.partial(kernel, pairs=pairs, spread=spread, devi...]
    add x3 -> x0, other arithmetic: 2.72 us -> none  [the longest x2 2.01 us: pair_ids(): key = target * pairs + slots]
    unnamed x2 -> x1, local copies, waits for them, and re-layouts: 3.47 us -> 2.06 us
    concatenate x1 -> x0, local copies, waits for them, and re-layouts: 1.32 us -> none  [pair_ids(): jnp.concatenate([by_source, jnp.minimum(by_target, panels - 1), keep, ord...]
    reduce_sum x4 -> x0, other arithmetic: 1.25 us -> none  [the longest x1 0.76 us: pair_ids(): jnp.sum(jnp.where(order[None, :] == rows[:, None], rows[None, :], 0), 1)]
    dynamic_slice x1 -> x0, local copies, waits for them, and re-layouts: 1.24 us -> none  [on_device(): near_count[device]]
where the time goes in v2:
time: 40.1 us; the launch traced here: 39.9 us
  Pallas kernels  37.9 us (95%)
  local copies, waits for them, and re-layouts  2.06 us (5%)
    pallas_call x1, Pallas kernels, on_device(): pl.pallas_call(functools.partial(kernel, pairs=pairs, spread=spread, devi...  37.9 us
    unnamed x1, local copies, waits for them, and re-layouts  2.06 us

profile of v2, /device:TPU:1, one launch (start us, length us, event | category | flops | bytes accessed | tf_op | source)
XLA Modules:
  0.0 39.9 jit_solution(15472883366319861882)
XLA Ops:
  0.0 37.9 %shard_map.100 = f32[48,32,128]{2,1,0:T(8,128)} custom-call(s32[1,48]{1,0:T(1,128)} %order_hbm.1, s32[16,144]{1,0:T(8,128)} %near_target_hbm.1, s32[16,144]{1,0:T(8,128)} %near_source_hbm.1, s32[16]{0:T(128)} %near_count_hbm.1, f32[48,32,128]{2,1,0:T(8,128)} %bitcast.8, f32[48,128]{1,0:T(8,128)} %weight_hbm.1, bf16[144,128]{1,0:T(8,128)(2,1)} %bitcast.9, ...), custom_call_target="tpu_custom_call" | custom-call | tf_op jit(solution)/shard_map/pallas_call | solution.py:576
  37.9 2.1 %copy.12 = f32[48,2,16,128]{3,2,1,0:T(8,128)} copy(f32[48,2,16,128]{3,2,1,0:T(8,128)} %bitcast.7) | data formatting | bytes 1572864
